TPU v7x, 128 devices: a whole 4x4x4 slice. The times are simulated.
128 devices in a mesh: dp: 8 (over y_lo, z), factor: 16 (over x, y_hi, core).
Axes of the slice: x: 4, y: 4 (y_hi: 2, y_lo: 2; y = y_hi * 2 + y_lo), z: 4, core: 2. Of those that a mesh axis runs over, the one named last changes fastest.
Arguments:
- inputs: bfloat16 [3072, 16384], P('dp'), may hold values from -6 to 6
- first_factor: bfloat16 [16384, 2048], P(None, 'factor'), may hold values from -0.046875 to 0.046875
- second_factor: bfloat16 [2048, 26624], P('factor'), may hold values from -0.125 to 0.125
- out_grad: bfloat16 [3072, 26624], P('dp', 'factor'), may hold values from -0.59765625 to 0.59765625
Outputs:
- input_grad: bfloat16 [3072, 16384], P('dp', 'factor')
- first_grad: bfloat16 [16384, 2048], P('dp', 'factor')
- second_grad: bfloat16 [2048, 26624], P('factor', 'dp')
All inputs are finite; a program needn't handle non-finite values.
Results may differ from a plain program's by a relative error of at most 0.023.
Values may be sent and summed in bfloat16 or wider, within the bound.
A program may use at most 192 MiB of HBM per device.

v0:
```python
import jax
import jax.numpy as jnp
from jax import lax
from jax.sharding import PartitionSpec as P


def contract_rows(left, right):
    return lax.dot_general(
        left, right, (((0,), (0,)), ((), ())), preferred_element_type=jnp.float32
    )


def contract_cols(left, right):
    return lax.dot_general(
        left, right, (((1,), (1,)), ((), ())), preferred_element_type=jnp.float32
    )


def shards(inputs, first_factor, second_factor, out_grad):
    hidden = jnp.dot(inputs, first_factor, preferred_element_type=jnp.float32).astype(jnp.bfloat16)
    piece = lax.all_gather(out_grad, "factor", axis=1, tiled=True)
    columns = second_factor
    rank_total = contract_cols(piece, columns)
    block = contract_rows(hidden, piece)
    second_terms = block
    rank_total, second_terms = (rank_total, second_terms)
    rank_grad = rank_total.astype(jnp.bfloat16)
    second_grad = lax.psum_scatter(
        second_terms.astype(jnp.bfloat16), "dp", scatter_dimension=1, tiled=True
    )
    columns = inputs
    first_grad = lax.psum_scatter(
        contract_rows(columns, rank_grad).astype(jnp.bfloat16),
        "dp",
        scatter_dimension=0,
        tiled=True,
    )
    partial_terms = contract_cols(rank_grad, first_factor)
    input_grad = lax.psum_scatter(
        partial_terms.astype(jnp.bfloat16), "factor", scatter_dimension=1, tiled=True
    )
    return (input_grad, first_grad, second_grad)


def solution(mesh):
    in_specs = (P("dp", None), P(None, "factor"), P("factor", None), P("dp", "factor"))
    out_specs = (P("dp", "factor"), P("dp", "factor"), P("factor", "dp"))
    return jax.shard_map(shards, mesh=mesh, in_specs=in_specs, out_specs=out_specs, check_vma=False)
```

profile of v0, /device:TPU:5, one launch (start us, length us, event | category | flops | bytes accessed | tf_op | source)
XLA Modules:
  0.0 421.7 jit_solution(1062345992108022976)
XLA Ops:
  7.2 0.0 all-gather.2.cloned.1.call-start
  7.2 0.7 all-gather.2.cloned.1.call-update
  7.9 0.0 reduce-scatter.6.cloned.1.call-start
  7.9 130.4 %all-gather.2.cloned.1.call-done = bf16[384,26624]{1,0:T(8,128)(2,1)} async-done(((bf16[384,1664]{1,0:T(8,128)(2,1)}), bf16[384,26624]{1,0:T(8,128)(2,1)}) %all-gather.2.cloned.1.call-update) | async-done | bytes 20447248 | tf_op jit(solution)/shard_map/all_gather | solution.py:21
  138.3 11.6 %convolution_convert_fusion.4 = bf16[384,128]{1,0:T(8,128)(2,1)S(1)} fusion(bf16[384,26624]{1,0:T(8,128)(2,1)} %all-gather.2.cloned.1.call-done, bf16[128,26624]{1,0:T(8,128)(2,1)} %param.6), kind=kOutput, calls=%fused_computation.5 | convolution fusion | flops 2617294848 | bytes 27361280 | tf_op jit(solution)/shard_map/dot_general | solution.py:14
  149.9 0.0 copy-start
  149.9 0.6 copy-done
  150.5 9.0 %fusion = bf16[16384,128]{0,1:T(8,128)(2,1)} fusion(bf16[384,128]{1,0:T(8,128)(2,1)S(1)} %convolution_convert_fusion.4, bf16[384,16384]{1,0:T(8,128)(2,1)} %param.4), kind=kOutput, calls=%fused_computation.3 | convolution fusion | flops 1612709888 | bytes 16875520 | tf_op jit(solution)/shard_map/dot_general | solution.py:8
  159.6 0.0 reduce-scatter.6.cloned.1.call-update
  159.6 0.2 reduce-scatter.8.cloned.1.call-start
  159.8 0.0 copy-start.1
  159.8 28.5 %convolution_convert_fusion = bf16[128,26624]{1,0:T(8,128)(2,1)} fusion(bf16[384,26624]{1,0:T(8,128)(2,1)} %all-gather.2.cloned.1.call-done, bf16[384,16384]{1,0:T(8,128)(2,1)} %param.4, bf16[16384,128]{1,0:T(8,128)(2,1)} %param.5), kind=kOutput, calls=%fused_computation | convolution fusion | flops 4231315456 | bytes 44040192 | tf_op jit(solution)/shard_map/dot_general | solution.py:8
  188.3 0.0 reduce-scatter.8.cloned.1.call-update
  188.3 0.0 reduce-scatter.4.cloned.1.call-start
  188.4 0.0 copy-done.1
  188.4 8.7 %convolution_convert_fusion.1 = bf16[384,16384]{1,0:T(8,128)(2,1)} fusion(bf16[384,128]{1,0:T(8,128)(2,1)S(1)} %copy-done.1, bf16[16384,128]{1,0:T(8,128)(2,1)} %param.5), kind=kOutput, calls=%fused_computation.1 | convolution fusion | flops 1616904192 | bytes 16875520 | tf_op jit(solution)/shard_map/dot_general | solution.py:14
  197.1 0.0 reduce-scatter.4.cloned.1.call-update
  197.1 15.0 %reduce-scatter.6.cloned.1.call-done = bf16[2048,128]{0,1:T(8,128)(2,1)} async-done(((bf16[16384,128]{0,1:T(8,128)(2,1)}), bf16[2048,128]{0,1:T(8,128)(2,1)}) %reduce-scatter.6.cloned.1.call-update) | async-done | bytes 524304 | tf_op jit(solution)/shard_map/reduce_scatter | solution.py:32
  212.1 2.0 copy.7
  214.1 77.7 %reduce-scatter.8.cloned.1.call-done = bf16[128,3328]{1,0:T(8,128)(2,1)} async-done(((bf16[128,26624]{1,0:T(8,128)(2,1)}), bf16[128,3328]{1,0:T(8,128)(2,1)}) %reduce-scatter.8.cloned.1.call-update) | async-done | bytes 851984 | tf_op jit(solution)/shard_map/reduce_scatter | solution.py:28
  291.8 123.4 %reduce-scatter.4.cloned.1.call-done = bf16[384,1024]{1,0:T(8,128)(2,1)} async-done(((bf16[384,16384]{1,0:T(8,128)(2,1)}), bf16[384,1024]{1,0:T(8,128)(2,1)}) %reduce-scatter.4.cloned.1.call-update) | async-done | bytes 786448 | tf_op jit(solution)/shard_map/reduce_scatter | solution.py:39
Async XLA Ops:
  7.2 131.1 %all-gather.2.cloned.1.call-start = ((), (), s32[]{:S(2)}) async-start(), calls=%async_computation.3 | async-start | bytes 21725184 | tf_op jit(solution)/shard_map/all_gather | solution.py:21
  7.9 204.2 %reduce-scatter.6.cloned.1.call-start = ((), (), s32[]{:S(2)}) async-start(), calls=%async_computation.5 | async-start | bytes 4718592 | tf_op jit(solution)/shard_map/reduce_scatter | solution.py:32
  149.9 0.6 copy-start
  159.6 132.2 %reduce-scatter.8.cloned.1.call-start = ((), (), s32[]{:S(2)}) async-start(), calls=%async_computation.6 | async-start | bytes 7667712 | tf_op jit(solution)/shard_map/reduce_scatter | solution.py:28
  159.8 28.6 %copy-start.1 = (bf16[384,128]{1,0:T(8,128)(2,1)S(1)}, bf16[384,128]{1,0:T(8,128)(2,1)}, u32[]{:S(2)}) copy-start(bf16[384,128]{1,0:T(8,128)(2,1)} %copy-done) | copy-start | bytes 294916
  188.3 226.8 %reduce-scatter.4.cloned.1.call-start = ((), (), s32[]{:S(2)}) async-start(), calls=%async_computation.4 | async-start | bytes 13369344 | tf_op jit(solution)/shard_map/reduce_scatter | solution.py:39
Sparse Core Ops, SparseCore 0:
  10.3 127.9 all-gather.1
  159.7 52.3 reduce-scatter.5
  215.1 76.6 reduce-scatter.7
  296.6 118.5 reduce-scatter.3
where the time goes:
time: 424 us; the launch traced here: 422 us
  waiting for transfers between devices  347 us (82%)
  matrix products  57.8 us (14%)
  between operations  13.8 us (3%)
    all_gather x1, waiting for transfers between devices, shards(): piece = lax.all_gather(out_grad, 'factor', axis=1, tiled=True)  130 us
    reduce_scatter x1, waiting for transfers between devices, shards(): lax.psum_scatter(partial_terms.astype(jnp.bfloat16), 'factor', scatter_di...  123 us
    reduce_scatter x1, waiting for transfers between devices, shards(): lax.psum_scatter(second_terms.astype(jnp.bfloat16), 'dp', scatter_dimensi...  77.7 us
    dot_general x2, matrix products, contract_rows(): lax.dot_general(left, right, (((0,), (0,)), ((), ())), preferred_element_...  37.5 us
    dot_general x2, matrix products, contract_cols(): lax.dot_general(left, right, (((1,), (1,)), ((), ())), preferred_element_...  20.3 us
    reduce_scatter x1, waiting for transfers between devices, shards(): lax.psum_scatter(contract_rows(columns, rank_grad).astype(jnp.bfloat16),...  15 us
  transfers between devices with their start and end apart: 4, of which 4 were waited for; matrix products, arithmetic and copies ran while one was open for 9% of the time, Pallas kernels for 0%

commit v1 on v0

v1 whole, which is shorter than its diff:
```python
import functools

import jax
import jax.numpy as jnp
from jax import lax
from jax.experimental import pallas as pl
from jax.experimental.pallas import tpu as pltpu
from jax.sharding import PartitionSpec as P

MESH = pl.DeviceIdType.MESH
BF = jnp.bfloat16
F32 = jnp.float32
TOK = 384
D = 16384
RK = 128
CB = 1664
FB = 1024
DB = 2048


def ds(i, n):
    return pl.ds(pl.multiple_of(i * n, n), n)


def nn(a, b):
    return jnp.dot(a, b, preferred_element_type=F32)


def nt(a, b):
    return lax.dot_general(a, b, (((1,), (1,)), ((), ())), preferred_element_type=F32)


def kernel(
    inp, ff, sf, og,
    ig_out, fg_out, sg_out,
    i_v, ff_v, og_r, sf_r, ffx, ht, h_acc, rg_acc, rg_p, rg_r, rg_all,
    sg_p, sg_r, sg_s, fg_p, fg_r, ig_p, ig_r, rgt,
    i_sem, ff_sem,
    og_ss, og_rs, sf_ss, sf_rs, fx_ss, fx_rs, h_ss, h_rs, rg_ss, rg_rs, ra_ss, ra_rs,
    sg_ss, sg_rs, c8_ss, c8_rs, fg_ss, fg_rs, ig_ss, ig_rs,
):
    d = lax.axis_index("dp")
    f = lax.axis_index("factor")
    yl, z = d // 4, d % 4
    x, yh, c = f // 4, (f // 2) % 2, f % 2
    y = 2 * yh + yl
    r4 = yh * 2 + c
    line = y * 2 + c

    def dev(x_, y_, z_, c_):
        return ((y_ % 2) * 4 + z_, x_ * 4 + (y_ // 2) * 2 + c_)

    def remote(src, dst, ss, rs, to):
        return pltpu.make_async_remote_copy(
            src_ref=src, dst_ref=dst, send_sem=ss, recv_sem=rs, device_id=to, device_id_type=MESH
        )

    def arrived(dst, rs):
        pltpu.make_async_copy(dst, dst, rs).wait()

    c8_to = [(x, 2 * (z // 2) + s, 2 * c + yh, z % 2) for s in range(2)]
    c8_from = [(x, 2 * (z % 2) + s, 2 * yh + c, z // 2) for s in range(2)]

    def is_me(t):
        return (t[1] == y) & (t[2] == z) & (t[3] == c)

    barrier = pltpu.get_barrier_semaphore()

    def greet(*t):
        pl.semaphore_signal(barrier, inc=1, device_id=dev(*t), device_id_type=MESH)

    for j in range(1, 8):
        other = (line + j) % 8
        greet(x, other // 2, z, other % 2)
    for k in range(1, 4):
        for yy in range(2):
            for cc in range(2):
                greet((x + k) % 4, 2 * yh + yy, z, cc)
    for k in range(1, 4):
        for yy in range(2):
            greet(x, 2 * yh + yy, (z + k) % 4, c)
    extra = 0
    for t in c8_to + c8_from:
        away = jnp.logical_not(is_me(t))

        @pl.when(away)
        def _(t=t):
            greet(*t)

        extra = extra + away.astype(jnp.int32)
    pl.semaphore_wait(barrier, 25 + extra)

    og_self = (c == yl) & (x % 2 == c)
    og_dst = og_r.at[ds(yl, TOK), ds(x // 2, CB)]
    og_rsem = og_rs.at[(x // 2) * 2 + yl]
    og_copies = [
        remote(og, og_dst, og_ss.at[k], og_rsem, dev((x + k) % 4, 2 * yh + c, z, x % 2))
        for k in range(4)
    ]
    og_local = pltpu.make_async_copy(og, og_dst, og_rsem)
    for k in (2, 1, 3):
        og_copies[k].start()

    @pl.when(jnp.logical_not(og_self))
    def _():
        og_copies[0].start()

    @pl.when(og_self)
    def _():
        og_local.start()

    ff_loads = [pltpu.make_async_copy(ff.at[k], ff_v.at[k], ff_sem.at[k]) for k in range(4)]
    i_loads = [
        pltpu.make_async_copy(inp.at[:, k * 4096 : (k + 1) * 4096], i_v.at[:, k * 4096 : (k + 1) * 4096], i_sem.at[k])
        for k in range(4)
    ]
    for k in range(4):
        ff_loads[k].start()
        i_loads[k].start()

    sends = []
    peers = [(y, 1 - c), (3 - y, 0), (3 - y, 1)]

    def sf_src(y_, c_, s):
        return sf.at[:, ds((2 * s + c_) * 4 + (y_ // 2) * 2 + y_ % 2, CB)]

    def sf_dst(s):
        return sf_r.at[ds(r4, RK), s * CB : (s + 1) * CB]

    for s in range(2):
        pltpu.make_async_copy(sf_src(y, c, s), sf_dst(s), sf_rs.at[r4 * 2 + s]).start()
        for n, (y_, c_) in enumerate(peers):
            cp = remote(sf_src(y_, c_, s), sf_dst(s), sf_ss.at[n * 2 + s], sf_rs.at[r4 * 2 + s], dev(x, y_, z, c_))
            cp.start()
            sends.append(cp)

    for k in range(4):
        ff_loads[k].wait()
        i_loads[k].wait()

        def h_step(j, _, k=k):
            h_acc[...] += nn(i_v[:, ds(k * 4 + j, FB)], ff_v[k, j])
            return 0

        if k == 0:
            h_acc[...] = jnp.zeros_like(h_acc)
        lax.fori_loop(0, 4, h_step, 0)
    ht_mine = ht.at[ds(r4, RK), ds(yl, TOK)]
    ht_mine[...] = h_acc[...].T.astype(BF)
    for j in range(1, 8):
        other = (line + j) % 8
        cp = remote(ht_mine, ht_mine, h_ss.at[j], h_rs.at[line], dev(x, other // 2, z, other % 2))
        cp.start()
        sends.append(cp)

    def fx_dst():
        return ffx.at[:, :, ds(r4, RK)]

    pltpu.make_async_copy(ff.at[:, r4], fx_dst(), fx_rs.at[r4]).start()
    for n, (y_, c_) in enumerate(peers):
        cp = remote(ff.at[:, (y_ // 2) * 2 + c_], fx_dst(), fx_ss.at[n], fx_rs.at[r4], dev(x, y_, z, c_))
        cp.start()
        sends.append(cp)

    for s in range(2):
        for q in range(4):
            arrived(sf_r.at[q * RK : (q + 1) * RK, s * CB : (s + 1) * CB], sf_rs.at[q * 2 + s])

    def rg_block(s):
        for t in range(2):
            arrived(og_r.at[t * TOK : (t + 1) * TOK, s * CB : (s + 1) * CB], og_rs.at[s * 2 + t])

            def step(n, _, t=t):
                part = nt(og_r[t * TOK : (t + 1) * TOK, s * CB : (s + 1) * CB], sf_r[ds(n, 256), s * CB : (s + 1) * CB])
                if s == 0:
                    rg_acc[t, n] = part
                else:
                    rg_p[t, :, ds(n, 256)] = (rg_acc[t, n] + part).astype(BF)
                return 0

            lax.fori_loop(0, 2, step, 0)

    def sg_block(s):
        def step(k, _):
            q = (z + k) % 4
            sg_p[q, :, s * CB : (s + 1) * CB] = nn(ht[ds(q, RK), :], og_r[:, s * CB : (s + 1) * CB]).astype(BF)

            @pl.when(k != 0)
            def _():
                remote(
                    sg_p.at[q, :, s * CB : (s + 1) * CB], sg_r.at[z, :, s * CB : (s + 1) * CB],
                    sg_ss.at[k * 2 + s], sg_rs.at[z * 2 + s], dev(x, y, q, c),
                ).start()

            return 0

        lax.fori_loop(0, 4, step, 0)

    rg_block(0)
    for j in range(1, 8):
        other = (line + j) % 8
        y_, c_ = other // 2, other % 2
        arrived(ht.at[ds((y_ // 2) * 2 + c_, RK), ds(y_ % 2, TOK)], h_rs.at[other])
    sg_block(0)
    rg_block(1)
    for j in range(1, 8):
        other = (line + j) % 8
        y_, c_ = other // 2, other % 2
        cp = remote(
            rg_p.at[y_ % 2, :, ds((y_ // 2) * 2 + c_, RK)], rg_r.at[line], rg_ss.at[j], rg_rs.at[line],
            dev(x, y_, z, c_),
        )
        cp.start()
        sends.append(cp)
    sg_block(1)

    total = rg_p[yl, :, ds(r4, RK)].astype(F32)
    for j in range(1, 8):
        other = (line + j) % 8
        arrived(rg_r.at[other], rg_rs.at[other])
        total = total + rg_r[other].astype(F32)
    rg_mine = rg_all.at[:, ds(r4, RK)]
    rg_mine[...] = total.astype(BF)
    for n, (y_, c_) in enumerate([(y, 1 - c), ((y + 2) % 4, 0), ((y + 2) % 4, 1)]):
        cp = remote(rg_mine, rg_mine, ra_ss.at[n], ra_rs.at[r4], dev(x, y_, z, c_))
        cp.start()
        sends.append(cp)
    rgt[...] = total.T.astype(BF)

    def fg_step(k, _):
        to = (d + k) % 8
        fg_p[to] = nn(rgt[...], i_v[:, ds(to, DB)]).astype(BF)

        @pl.when(k != 8)
        def _():
            remote(fg_p.at[to], fg_r.at[d], fg_ss.at[k - 1], fg_rs.at[d], (to, f)).start()

        return 0

    lax.fori_loop(1, 9, fg_step, 0)

    for j in range(4):
        arrived(ffx.at[:, :, j * RK : (j + 1) * RK], fx_rs.at[j])
    for j in range(1, 4):
        other = (r4 + j) % 4
        arrived(rg_all.at[:, ds(other, RK)], ra_rs.at[other])

    def ig_step(k, _):
        to = (x + k) % 4
        ig_p[to] = nt(rg_all[...], ffx[to]).astype(BF)

        @pl.when(k != 4)
        def _():
            remote(ig_p.at[to], ig_r.at[x], ig_ss.at[k - 1], ig_rs.at[x], dev(to, y, z, c)).start()

        return 0

    lax.fori_loop(1, 5, ig_step, 0)

    c8_copies = []
    for s in range(2):
        cols = slice(s * CB, (s + 1) * CB)
        total = sg_p[z, :, cols].astype(F32)
        for j in range(1, 4):
            other = (z + j) % 4
            arrived(sg_r.at[other, :, cols], sg_rs.at[other * 2 + s])
            total = total + sg_r[other, :, cols].astype(F32)
        sg_s[:, cols] = total.astype(BF)
        dst = sg_out.at[:, ds(yl, CB)]
        far = remote(sg_s.at[:, cols], dst, c8_ss.at[s], c8_rs.at[yl], dev(*c8_to[s]))
        near = pltpu.make_async_copy(sg_s.at[:, cols], dst, c8_rs.at[yl])

        @pl.when(jnp.logical_not(is_me(c8_to[s])))
        def _(far=far):
            far.start()

        @pl.when(is_me(c8_to[s]))
        def _(near=near):
            near.start()

        c8_copies.append(far)

    for j in range(1, 4):
        other = (x + j) % 4
        arrived(ig_r.at[other], ig_rs.at[other])

    def ig_sum(k, _):
        rows = ds(k, 64)
        acc = ig_p[x, rows, :].astype(F32)
        for j in range(1, 4):
            acc = acc + ig_r[(x + j) % 4, rows, :].astype(F32)
        ig_out[rows, :] = acc.astype(BF)
        return 0

    lax.fori_loop(0, TOK // 64, ig_sum, 0)

    for j in range(1, 8):
        other = (d + j) % 8
        arrived(fg_r.at[other], fg_rs.at[other])

    def fg_sum(k, _):
        cols = ds(k, 256)
        acc = fg_p[d, :, cols].astype(F32)
        for j in range(1, 8):
            acc = acc + fg_r[(d + j) % 8, :, cols].astype(F32)
        fg_out[cols, :] = acc.T.astype(BF)
        return 0

    lax.fori_loop(0, DB // 256, fg_sum, 0)

    for s in range(2):
        arrived(sg_out.at[:, s * CB : (s + 1) * CB], c8_rs.at[s])

    for cp in sends:
        cp.wait_send()
    for k in range(1, 4):
        og_copies[k].wait_send()

    @pl.when(jnp.logical_not(og_self))
    def _():
        og_copies[0].wait_send()

    for s in range(2):

        @pl.when(jnp.logical_not(is_me(c8_to[s])))
        def _(s=s):
            c8_copies[s].wait_send()

        for k in range(1, 4):
            cols = slice(s * CB, (s + 1) * CB)
            q = (z + k) % 4
            remote(
                sg_p.at[q, :, cols], sg_r.at[z, :, cols], sg_ss.at[k * 2 + s], sg_rs.at[z * 2 + s], dev(x, y, q, c)
            ).wait_send()
    for k in range(1, 8):
        to = (d + k) % 8
        remote(fg_p.at[to], fg_r.at[d], fg_ss.at[k - 1], fg_rs.at[d], (to, f)).wait_send()
    for k in range(1, 4):
        to = (x + k) % 4
        remote(ig_p.at[to], ig_r.at[x], ig_ss.at[k - 1], ig_rs.at[x], dev(to, y, z, c)).wait_send()


def shards(inputs, first_factor, second_factor, out_grad):
    ff = first_factor.reshape(4, 4, FB, RK)
    any_ = pl.BlockSpec(memory_space=pl.ANY)
    vmem = pl.BlockSpec(memory_space=pltpu.VMEM)
    dma = pltpu.SemaphoreType.DMA
    return pl.pallas_call(
        kernel,
        name="backward",
        out_shape=(
            jax.ShapeDtypeStruct((TOK, FB), BF),
            jax.ShapeDtypeStruct((DB, RK), BF),
            jax.ShapeDtypeStruct((RK, 2 * CB), BF),
        ),
        in_specs=[any_] * 4,
        out_specs=(vmem, vmem, vmem),
        scratch_shapes=[
            pltpu.VMEM((TOK, D), BF),
            pltpu.VMEM((4, 4, FB, RK), BF),
            pltpu.VMEM((2 * TOK, 2 * CB), BF),
            pltpu.VMEM((4 * RK, 2 * CB), BF),
            pltpu.VMEM((4, FB, 4 * RK), BF),
            pltpu.VMEM((4 * RK, 2 * TOK), BF),
            pltpu.VMEM((TOK, RK), F32),
            pltpu.VMEM((2, 2, TOK, 256), F32),
            pltpu.VMEM((2, TOK, 4 * RK), BF),
            pltpu.VMEM((8, TOK, RK), BF),
            pltpu.VMEM((TOK, 4 * RK), BF),
            pltpu.VMEM((4, RK, 2 * CB), BF),
            pltpu.VMEM((4, RK, 2 * CB), BF),
            pltpu.VMEM((RK, 2 * CB), BF),
            pltpu.VMEM((8, RK, DB), BF),
            pltpu.VMEM((8, RK, DB), BF),
            pltpu.VMEM((4, TOK, FB), BF),
            pltpu.VMEM((4, TOK, FB), BF),
            pltpu.VMEM((RK, TOK), BF),
            dma((4,)), dma((4,)),
            dma((4,)), dma((4,)),
            dma((6,)), dma((8,)),
            dma((3,)), dma((4,)),
            dma((8,)), dma((8,)),
            dma((8,)), dma((8,)),
            dma((3,)), dma((4,)),
            dma((8,)), dma((8,)),
            dma((2,)), dma((2,)),
            dma((7,)), dma((8,)),
            dma((3,)), dma((4,)),
        ],
        cost_estimate=pl.CostEstimate(flops=10_100_000_000, bytes_accessed=30_000_000, transcendentals=0),
        compiler_params=pltpu.CompilerParams(
            collective_id=0, has_side_effects=True, vmem_limit_bytes=63 * 1024 * 1024
        ),
    )(inputs, ff, second_factor, out_grad)


def solution(mesh):
    in_specs = (P("dp", None), P(None, "factor"), P("factor", None), P("dp", "factor"))
    out_specs = (P("dp", "factor"), P("dp", "factor"), P("factor", "dp"))
    return jax.shard_map(shards, mesh=mesh, in_specs=in_specs, out_specs=out_specs, check_vma=False)
```

time: 424 us -> 203 us (0.48)
  the two profiles are of different devices: /device:TPU:5 before, /device:TPU:48 now
where the time goes in v1:
time: 203 us
  Pallas kernels  196 us (97%)
  local copies, waits for them, and re-layouts  6.04 us (3%)
    pallas_call x1, Pallas kernels, shards(): pl.pallas_call(kernel, name='backward', out_shape=(jax.ShapeDtypeStruct((...  196 us
    unnamed x3, local copies, waits for them, and re-layouts  6.04 us

profile of v1, /device:TPU:48, one launch (start us, length us, event | category | flops | bytes accessed | tf_op | source)
XLA Modules:
  0.0 202.9 jit_solution(16886160243597386407)
XLA Ops:
  0.6 196.2 %backward.1 = (bf16[384,1024]{1,0:T(8,128)(2,1)}, bf16[2048,128]{1,0:T(8,128)(2,1)}, bf16[128,3328]{1,0:T(8,128)(2,1)}) custom-call(bf16[384,16384]{1,0:T(8,128)(2,1)} %inp.1, bf16[4,4,1024,128]{3,2,1,0:T(8,128)(2,1)} %bitcast.1, bf16[128,26624]{1,0:T(8,128)(2,1)} %sf.1, bf16[384,1664]{1,0:T(8,128)(2,1)} %og.1), custom_call_target="tpu_custom_call" | custom-call | flops 10099999744 | bytes 30000000 | tf_op jit(solution)/shard_map/backward/pallas_call | solution.py:348
  196.8 2.1 %copy.10 = bf16[384,1024]{1,0:T(8,128)(2,1)} copy(bf16[384,1024]{1,0:T(8,128)(2,1)} %get-tuple-element.6) | data formatting | bytes 1572864
  198.9 1.9 copy.11
  200.8 2.1 %copy.12 = bf16[128,3328]{1,0:T(8,128)(2,1)} copy(bf16[128,3328]{1,0:T(8,128)(2,1)} %get-tuple-element.8) | data formatting | bytes 1703936

commit v2 on v1

v2 whole, which is shorter than its diff:
```python
import functools

import jax
import jax.numpy as jnp
from jax import lax
from jax.experimental import pallas as pl
from jax.experimental.pallas import tpu as pltpu
from jax.sharding import PartitionSpec as P

MESH = pl.DeviceIdType.MESH
BF = jnp.bfloat16
F32 = jnp.float32
TOK = 384
D = 16384
RK = 128
CB = 1664
FB = 1024
DB = 2048


def ds(i, n):
    return pl.ds(pl.multiple_of(i * n, n), n)


def nn(a, b):
    return jnp.dot(a, b, preferred_element_type=F32)


def nt(a, b):
    return lax.dot_general(a, b, (((1,), (1,)), ((), ())), preferred_element_type=F32)


def kernel(
    inp, ff, sf, og,
    ig_out, fg_out, sg_out,
    i_v, ff_v, og_r, sf_r, ffx, ht, h_acc, rg_acc, rg_p, rg_r, rg_all,
    sg_p, sg_r, sg_s, fg_p, fg_y, fg_z, fg_f, ig_p, ig_r, rgt,
    i_sem, ff_sem,
    og_ss, og_rs, fwd_ss, sf_ss, sf_rs, fx_ss, fx_rs, h_ss, h_rs, rg_ss, rg_rs, ra_ss, ra_rs,
    sg_ss, sg_rs, c8_ss, c8_rs, fy_ss, fy_rs, fz_ss, fz_rs, ff_ss, ff_rs, ig_ss, ig_rs,
):
    d = lax.axis_index("dp")
    f = lax.axis_index("factor")
    yl, z = d // 4, d % 4
    x, yh, c = f // 4, (f // 2) % 2, f % 2
    y = 2 * yh + yl
    yp = 2 * yh + 1 - yl
    r4 = yh * 2 + c
    line = y * 2 + c
    root = c == x % 2
    s0, s1 = x // 2, 1 - x // 2

    def dev(x_, y_, z_, c_):
        return ((y_ % 2) * 4 + z_, x_ * 4 + (y_ // 2) * 2 + c_)

    def remote(src, dst, ss, rs, to):
        return pltpu.make_async_remote_copy(
            src_ref=src, dst_ref=dst, send_sem=ss, recv_sem=rs, device_id=to, device_id_type=MESH
        )

    def arrived(dst, rs):
        pltpu.make_async_copy(dst, dst, rs).wait()

    sends = []

    def send(cp, cond=None):
        if cond is None:
            cp.start()
        else:
            pl.when(cond)(cp.start)
        sends.append((cond, cp))

    c8_to = [(x, 2 * (z // 2) + s, 2 * c + yh, z % 2) for s in range(2)]
    c8_from = [(x, 2 * (z % 2) + s, 2 * yh + c, z // 2) for s in range(2)]

    def is_me(t):
        return (t[1] == y) & (t[2] == z) & (t[3] == c)

    barrier = pltpu.get_barrier_semaphore()

    def greet(*t):
        pl.semaphore_signal(barrier, inc=1, device_id=dev(*t), device_id_type=MESH)

    for j in range(1, 8):
        other = (line + j) % 8
        greet(x, other // 2, z, other % 2)
    for k in range(1, 4):
        for cc in range(2):
            greet((x + k) % 4, y, z, cc)
    for k in range(1, 4):
        greet(x, y, (z + k) % 4, c)
    extra = 0
    for t in c8_to + c8_from:
        away = jnp.logical_not(is_me(t))

        @pl.when(away)
        def _(t=t):
            greet(*t)

        extra = extra + away.astype(jnp.int32)
    pl.semaphore_wait(barrier, 16 + extra)

    stays = c == yl
    moves = jnp.logical_not(stays)
    right, left = (x + 1) % 4, (x + 3) % 4
    og_dst = og_r.at[s0, ds(yl, TOK), :]
    og_rsem = og_rs.at[s0 * 2 + yl]
    send(remote(og, og_dst, og_ss.at[0], og_rsem, dev(right, y, z, x % 2)), stays)
    send(remote(og, og_dst, og_ss.at[1], og_rsem, dev(left, y, z, x % 2)), stays)
    send(remote(og, og_dst, og_ss.at[2], og_rsem, dev(x, yp, z, x % 2)), moves)
    send(remote(og, og_dst, og_ss.at[3], og_rsem, dev(x, y, z, 1 - c)), stays & jnp.logical_not(root))

    @pl.when(stays & root)
    def _():
        pltpu.make_async_copy(og, og_dst, og_rsem).start()

    ff_loads = [pltpu.make_async_copy(ff.at[k], ff_v.at[k], ff_sem.at[k]) for k in range(4)]
    i_loads = [
        pltpu.make_async_copy(inp.at[:, k * 4096 : (k + 1) * 4096], i_v.at[:, k * 4096 : (k + 1) * 4096], i_sem.at[k])
        for k in range(4)
    ]
    for k in range(4):
        ff_loads[k].start()
        i_loads[k].start()

    peers = [(y, 1 - c), (3 - y, 0), (3 - y, 1)]

    def sf_src(y_, c_, s):
        return sf.at[:, ds((2 * s + c_) * 4 + (y_ // 2) * 2 + y_ % 2, CB)]

    def sf_send(n, s):
        dst, rs = sf_r.at[s, ds(r4, RK), :], sf_rs.at[r4 * 2 + s]
        pltpu.make_async_copy(sf_src(y, c, s), dst, rs).start()
        for m, (y_, c_) in enumerate(peers):
            send(remote(sf_src(y_, c_, s), dst, sf_ss.at[m * 2 + n], rs, dev(x, y_, z, c_)))

    def fx_send(k):
        to = (x + k) % 4
        dst, rs = ffx.at[to, :, ds(r4, RK)], fx_rs.at[to * 4 + r4]
        pltpu.make_async_copy(ff.at[to, r4], dst, rs).start()
        for m, (y_, c_) in enumerate(peers):
            send(remote(ff.at[to, (y_ // 2) * 2 + c_], dst, fx_ss.at[m * 4 + k], rs, dev(x, y_, z, c_)))

    sf_send(0, s0)

    h_acc[...] = jnp.zeros_like(h_acc)
    for k in range(4):
        ff_loads[k].wait()
        i_loads[k].wait()

        def h_step(j, _, k=k):
            h_acc[...] += nn(i_v[:, ds(k * 4 + j, FB)], ff_v[k, j])
            return 0

        lax.fori_loop(0, 4, h_step, 0)
    ht_mine = ht.at[ds(r4, RK), ds(yl, TOK)]
    ht_mine[...] = h_acc[...].T.astype(BF)
    for j in range(1, 8):
        other = (line + j) % 8
        send(remote(ht_mine, ht_mine, h_ss.at[j], h_rs.at[line], dev(x, other // 2, z, other % 2)))

    sf_send(1, s1)
    fx_send(2)
    fx_send(1)

    rg_acc[...] = jnp.zeros_like(rg_acc)

    def sf_wait(s):
        for q in range(4):
            arrived(sf_r.at[s, q * RK : (q + 1) * RK, :], sf_rs.at[q * 2 + s])

    def block(s, t):
        arrived(og_r.at[s, ds(t, TOK), :], og_rs.at[s * 2 + t])

    def rg_block(s, t):
        def step(n, _):
            rg_acc[t, n] += nt(og_r[s, ds(t, TOK), :], sf_r[s, ds(n, 256), :])
            return 0

        lax.fori_loop(0, 2, step, 0)

    def sg_copy(k, s):
        q = (z + k) % 4
        return remote(sg_p.at[s, q], sg_r.at[s, z], sg_ss.at[k * 2 + s], sg_rs.at[z * 2 + s], dev(x, y, q, c))

    def sg_block(s):
        def step(i, _):
            k = (i + 2) % 4
            q = (z + k) % 4
            sg_p[s, q] = nn(ht[ds(q, RK), :], og_r[s]).astype(BF)

            @pl.when(k != 0)
            def _():
                sg_copy(k, s).start()

            return 0

        lax.fori_loop(0, 4, step, 0)

    def pick(u, v):
        return jnp.where(root, u, v)

    def onward(i, s, t):
        src = og_r.at[s, ds(t, TOK), :]
        from_left = (2 * s + c) == left
        mine = root & (s == s0) & (t != yl)
        ahead = jnp.logical_not(root) & (t == 0) & from_left
        back = jnp.logical_not(root) & (t == 1) & jnp.logical_not(from_left)
        rs = og_rs.at[s * 2 + t]
        send(remote(src, src, fwd_ss.at[i * 2], rs, dev(right, y, z, c)), mine | ahead)
        send(remote(src, src, fwd_ss.at[i * 2 + 1], rs, dev(left, y, z, c)), mine | back)

    order = [(s0, yl), (pick(s0, s1), pick(1 - yl, yl)), (pick(s1, s0), pick(yl, 1 - yl)), (s1, 1 - yl)]
    block(*order[0])
    onward(0, *order[0])
    block(*order[1])
    onward(1, *order[1])
    sf_wait(s0)
    rg_block(*order[0])
    sf_wait(s1)
    rg_block(*order[1])
    for j in range(1, 8):
        other = (line + j) % 8
        y_, c_ = other // 2, other % 2
        arrived(ht.at[ds((y_ // 2) * 2 + c_, RK), ds(y_ % 2, TOK)], h_rs.at[other])

    @pl.when(root)
    def _():
        sg_block(s0)

    block(*order[2])
    onward(2, *order[2])
    rg_block(*order[2])
    block(*order[3])
    onward(3, *order[3])
    rg_block(*order[3])

    for t in range(2):
        for n in range(2):
            rg_p[t, :, n * 256 : (n + 1) * 256] = rg_acc[t, n].astype(BF)
    for j in range(1, 8):
        other = (line + j) % 8
        y_, c_ = other // 2, other % 2
        send(
            remote(
                rg_p.at[y_ % 2, :, ds((y_ // 2) * 2 + c_, RK)], rg_r.at[line], rg_ss.at[j], rg_rs.at[line],
                dev(x, y_, z, c_),
            )
        )

    @pl.when(jnp.logical_not(root))
    def _():
        sg_block(s0)

    sg_block(s1)

    total = rg_p[yl, :, ds(r4, RK)].astype(F32)
    for j in range(1, 8):
        other = (line + j) % 8
        arrived(rg_r.at[other], rg_rs.at[other])
        total = total + rg_r[other].astype(F32)
    rg_mine = rg_all.at[:, ds(r4, RK)]
    rg_mine[...] = total.astype(BF)
    for n, (y_, c_) in enumerate([(y, 1 - c), ((y + 2) % 4, 0), ((y + 2) % 4, 1)]):
        send(remote(rg_mine, rg_mine, ra_ss.at[n], ra_rs.at[r4], dev(x, y_, z, c_)))
    rgt[...] = total.T.astype(BF)
    fx_send(3)
    fx_send(0)

    def fg_unit(own, z_, half):
        u = (pick_yl(own) * 4 + z_) * 2 + half
        fg_p[u] = nn(rgt[...], i_v[:, ds(u, FB)]).astype(BF)
        return u

    def pick_yl(own):
        return yl if own else 1 - yl

    def z_copy(kind, u, k):
        to = (z + k) % 4
        return remote(fg_p.at[u], fg_z.at[kind, z], fz_ss.at[kind * 4 + k], fz_rs.at[kind * 4 + z], dev(x, y, to, c))

    def y_copy(u, z_):
        return remote(fg_p.at[u], fg_y.at[z_], fy_ss.at[z_], fy_rs.at[z_], dev(x, yp, z, c))

    def p2(i, _):
        z_ = (z + i + 2) % 4
        y_copy(fg_unit(False, z_, 1), z_).start()
        return 0

    lax.fori_loop(0, 4, p2, 0)
    for own in (False, True):

        def first(i, _, own=own):
            k = (i + 2) % 4
            u = fg_unit(own, (z + k) % 4, 0)

            @pl.when(k != 0)
            def _():
                z_copy(0 if own else 1, u, k).start()

            return 0

        lax.fori_loop(0, 4, first, 0)

    def o2(z_, _):
        fg_unit(True, z_, 1)
        return 0

    lax.fori_loop(0, 4, o2, 0)

    for j in range(1, 4):
        other = (r4 + j) % 4
        arrived(rg_all.at[:, ds(other, RK)], ra_rs.at[other])

    def ig_copy(k):
        to = (x + k) % 4
        return remote(ig_p.at[to], ig_r.at[x], ig_ss.at[k], ig_rs.at[x], dev(to, y, z, c))

    def ig_part(k):
        to = (x + k) % 4
        for j in range(4):
            arrived(ffx.at[to, :, j * RK : (j + 1) * RK], fx_rs.at[to * 4 + j])
        ig_p[to] = nt(rg_all[...], ffx[to]).astype(BF)
        if k:
            send(ig_copy(k))

    ig_part(2)
    ig_part(1)

    def merge(i, _):
        k = (i + 2) % 4
        z_ = (z + k) % 4
        u = (yl * 4 + z_) * 2 + 1
        arrived(fg_y.at[z_], fy_rs.at[z_])
        fg_p[u] = (fg_p[u].astype(F32) + fg_y[z_].astype(F32)).astype(BF)

        @pl.when(k != 0)
        def _():
            z_copy(2, u, k).start()

        return 0

    lax.fori_loop(0, 4, merge, 0)
    ig_part(3)
    ig_part(0)

    for s in range(2):
        for j in range(1, 4):
            other = (z + j) % 4
            arrived(sg_r.at[s, other], sg_rs.at[other * 2 + s])
        total = sg_p[s, z].astype(F32)
        for j in range(1, 4):
            total = total + sg_r[s, (z + j) % 4].astype(F32)
        sg_s[s] = total.astype(BF)
        dst = sg_out.at[:, ds(yl, CB)]
        near = pltpu.make_async_copy(sg_s.at[s], dst, c8_rs.at[yl])
        send(remote(sg_s.at[s], dst, c8_ss.at[s], c8_rs.at[yl], dev(*c8_to[s])), jnp.logical_not(is_me(c8_to[s])))
        pl.when(is_me(c8_to[s]))(near.start)

    for j in range(1, 4):
        other = (z + j) % 4
        arrived(fg_z.at[1, other], fz_rs.at[4 + other])
    total = fg_p[((1 - yl) * 4 + z) * 2].astype(F32)
    for j in range(1, 4):
        total = total + fg_z[1, (z + j) % 4].astype(F32)
    fg_f[0] = total.astype(BF)
    send(remote(fg_f.at[0], fg_f.at[1], ff_ss.at[0], ff_rs.at[0], dev(x, yp, z, c)))

    for j in range(1, 4):
        other = (x + j) % 4
        arrived(ig_r.at[other], ig_rs.at[other])

    def ig_sum(k, _):
        rows = ds(k, 64)
        acc = ig_p[x, rows, :].astype(F32)
        for j in range(1, 4):
            acc = acc + ig_r[(x + j) % 4, rows, :].astype(F32)
        ig_out[rows, :] = acc.astype(BF)
        return 0

    lax.fori_loop(0, TOK // 64, ig_sum, 0)

    for half in range(2):
        kind = 2 * half
        for j in range(1, 4):
            other = (z + j) % 4
            arrived(fg_z.at[kind, other], fz_rs.at[kind * 4 + other])
        if half == 0:
            arrived(fg_f.at[1], ff_rs.at[0])

        def fg_sum(k, _, half=half, kind=kind):
            cols = ds(k, 256)
            acc = fg_p[d * 2 + half, :, cols].astype(F32)
            for j in range(1, 4):
                acc = acc + fg_z[kind, (z + j) % 4, :, cols].astype(F32)
            if half == 0:
                acc = acc + fg_f[1, :, cols].astype(F32)
            fg_out[ds(half * 4 + k, 256), :] = acc.T.astype(BF)
            return 0

        lax.fori_loop(0, FB // 256, fg_sum, 0)

    for s in range(2):
        arrived(sg_out.at[:, s * CB : (s + 1) * CB], c8_rs.at[s])

    for cond, cp in sends:
        if cond is None:
            cp.wait_send()
        else:
            pl.when(cond)(cp.wait_send)
    for k in range(1, 4):
        for s in range(2):
            sg_copy(k, s).wait_send()
        z_ = (z + k) % 4
        z_copy(0, (yl * 4 + z_) * 2, k).wait_send()
        z_copy(1, ((1 - yl) * 4 + z_) * 2, k).wait_send()
        z_copy(2, (yl * 4 + z_) * 2 + 1, k).wait_send()
    for z_ in range(4):
        y_copy(((1 - yl) * 4 + z_) * 2 + 1, z_).wait_send()


def shards(inputs, first_factor, second_factor, out_grad):
    ff = first_factor.reshape(4, 4, FB, RK)
    any_ = pl.BlockSpec(memory_space=pl.ANY)
    vmem = pl.BlockSpec(memory_space=pltpu.VMEM)
    dma = pltpu.SemaphoreType.DMA
    return pl.pallas_call(
        kernel,
        name="backward",
        out_shape=(
            jax.ShapeDtypeStruct((TOK, FB), BF),
            jax.ShapeDtypeStruct((DB, RK), BF),
            jax.ShapeDtypeStruct((RK, 2 * CB), BF),
        ),
        in_specs=[any_] * 4,
        out_specs=(vmem, vmem, vmem),
        scratch_shapes=[
            pltpu.VMEM((TOK, D), BF),
            pltpu.VMEM((4, 4, FB, RK), BF),
            pltpu.VMEM((2, 2 * TOK, CB), BF),
            pltpu.VMEM((2, 4 * RK, CB), BF),
            pltpu.VMEM((4, FB, 4 * RK), BF),
            pltpu.VMEM((4 * RK, 2 * TOK), BF),
            pltpu.VMEM((TOK, RK), F32),
            pltpu.VMEM((2, 2, TOK, 256), F32),
            pltpu.VMEM((2, TOK, 4 * RK), BF),
            pltpu.VMEM((8, TOK, RK), BF),
            pltpu.VMEM((TOK, 4 * RK), BF),
            pltpu.VMEM((2, 4, RK, CB), BF),
            pltpu.VMEM((2, 4, RK, CB), BF),
            pltpu.VMEM((2, RK, CB), BF),
            pltpu.VMEM((16, RK, FB), BF),
            pltpu.VMEM((4, RK, FB), BF),
            pltpu.VMEM((3, 4, RK, FB), BF),
            pltpu.VMEM((2, RK, FB), BF),
            pltpu.VMEM((4, TOK, FB), BF),
            pltpu.VMEM((4, TOK, FB), BF),
            pltpu.VMEM((RK, TOK), BF),
            dma((4,)), dma((4,)),
            dma((4,)), dma((4,)), dma((8,)),
            dma((6,)), dma((8,)),
            dma((12,)), dma((16,)),
            dma((8,)), dma((8,)),
            dma((8,)), dma((8,)),
            dma((3,)), dma((4,)),
            dma((8,)), dma((8,)),
            dma((2,)), dma((2,)),
            dma((4,)), dma((4,)),
            dma((12,)), dma((12,)),
            dma((1,)), dma((1,)),
            dma((4,)), dma((4,)),
        ],
        cost_estimate=pl.CostEstimate(flops=10_100_000_000, bytes_accessed=30_000_000, transcendentals=0),
        compiler_params=pltpu.CompilerParams(
            collective_id=0, has_side_effects=True, vmem_limit_bytes=63 * 1024 * 1024
        ),
    )(inputs, ff, second_factor, out_grad)


def solution(mesh):
    in_specs = (P("dp", None), P(None, "factor"), P("factor", None), P("dp", "factor"))
    out_specs = (P("dp", "factor"), P("dp", "factor"), P("factor", "dp"))
    return jax.shard_map(shards, mesh=mesh, in_specs=in_specs, out_specs=out_specs, check_vma=False)
```

time: 203 us -> 160 us (0.79)
  the two profiles are of different devices: /device:TPU:48 before, /device:TPU:3 now
where the time goes in v2:
time: 160 us; the launch traced here: 159 us
  Pallas kernels  153 us (96%)
  local copies, waits for them, and re-layouts  6.04 us (4%)
    pallas_call x1, Pallas kernels, shards(): pl.pallas_call(kernel, name='backward', out_shape=(jax.ShapeDtypeStruct((...  153 us
    unnamed x3, local copies, waits for them, and re-layouts  6.04 us

profile of v2, /device:TPU:3, one launch (start us, length us, event | category | flops | bytes accessed | tf_op | source)
XLA Modules:
  0.0 159.4 jit_solution(17956038487904115407)
XLA Ops:
  0.6 152.7 %backward.1 = (bf16[384,1024]{1,0:T(8,128)(2,1)}, bf16[2048,128]{1,0:T(8,128)(2,1)}, bf16[128,3328]{1,0:T(8,128)(2,1)}) custom-call(bf16[384,16384]{1,0:T(8,128)(2,1)} %inp.1, bf16[4,4,1024,128]{3,2,1,0:T(8,128)(2,1)} %bitcast.1, bf16[128,26624]{1,0:T(8,128)(2,1)} %sf.1, bf16[384,1664]{1,0:T(8,128)(2,1)} %og.1), custom_call_target="tpu_custom_call" | custom-call | flops 10099999744 | bytes 30000000 | tf_op jit(solution)/shard_map/backward/pallas_call | solution.py:427
  153.4 2.1 %copy.10 = bf16[384,1024]{1,0:T(8,128)(2,1)} copy(bf16[384,1024]{1,0:T(8,128)(2,1)} %get-tuple-element.6) | data formatting | bytes 1572864
  155.4 1.9 %copy.11 = bf16[2048,128]{1,0:T(8,128)(2,1)} copy(bf16[2048,128]{1,0:T(8,128)(2,1)} %get-tuple-element.7) | data formatting | bytes 1048576
  157.3 2.1 %copy.12 = bf16[128,3328]{1,0:T(8,128)(2,1)} copy(bf16[128,3328]{1,0:T(8,128)(2,1)} %get-tuple-element.8) | data formatting | bytes 1703936

commit v3 on v2

--- a/solution.py
+++ b/solution.py
@@ -13,6 +13,7 @@
 TOK = 384
 D = 16384
 RK = 128
+QR = 32
 CB = 1664
 FB = 1024
 DB = 2048
@@ -34,9 +35,9 @@
     inp, ff, sf, og,
     ig_out, fg_out, sg_out,
     i_v, ff_v, og_r, sf_r, ffx, ht, h_acc, rg_acc, rg_p, rg_r, rg_all,
-    sg_p, sg_r, sg_s, fg_p, fg_y, fg_z, fg_f, ig_p, ig_r, rgt,
+    sg_p, sg_m, sg_r, sg_s, fg_p, fg_y, fg_m, fg_z, fg_f, ig_p, ig_m, ig_r, rgt,
     i_sem, ff_sem,
-    og_ss, og_rs, fwd_ss, sf_ss, sf_rs, fx_ss, fx_rs, h_ss, h_rs, rg_ss, rg_rs, ra_ss, ra_rs,
+    og_ss, og_rs, fwd_ss, sf_ss, sf_rs, sq_rs, fx_ss, fx_rs, fxh_rs, h_ss, h_rs, rg_ss, rg_rs, ra_ss, ra_rs,
     sg_ss, sg_rs, c8_ss, c8_rs, fy_ss, fy_rs, fz_ss, fz_rs, ff_ss, ff_rs, ig_ss, ig_rs,
 ):
     d = lax.axis_index("dp")
@@ -70,6 +71,54 @@
             pl.when(cond)(cp.start)
         sends.append((cond, cp))
 
+    class RingSum:
+        def __init__(self, at, to_dev, part, rows, mid, out, ss, rs, base):
+            far, up, down = (at + 2) % 4, (at + 1) % 4, (at + 3) % 4
+            lo, hi = pl.ds(0, rows // 2), pl.ds(rows // 2, rows // 2)
+
+            def cp(n, src, dst, to):
+                return remote(src, dst, ss.at[base + n], rs.at[base + n], to_dev(to))
+
+            self.mid = mid
+            self.far = [cp(0, part(far).at[lo], mid.at[0], up), cp(1, part(far).at[hi], mid.at[1], down)]
+            self.plain = [cp(2, part(up).at[hi], out.at[0, hi], up), cp(3, part(down).at[lo], out.at[1, lo], down)]
+            self.merged = [cp(4, part(up).at[lo], out.at[0, lo], up), cp(5, part(down).at[hi], out.at[1, hi], down)]
+            self.own = [part(up).at[lo], part(down).at[hi]]
+            self.mids = [(mid.at[0], rs.at[base]), (mid.at[1], rs.at[base + 1])]
+            self.outs = [
+                (out.at[0, hi], rs.at[base + 2]), (out.at[1, lo], rs.at[base + 3]),
+                (out.at[0, lo], rs.at[base + 4]), (out.at[1, hi], rs.at[base + 5]),
+            ]
+
+        def part_done(self, i):
+            pl.when(i == 0)(self.send_far)
+            pl.when(i == 1)(self.plain[1].start)
+            pl.when(i == 2)(self.plain[0].start)
+
+        def send_far(self):
+            self.far[0].start()
+            self.far[1].start()
+
+        def merge(self):
+            for n, own in enumerate(self.own):
+                arrived(*self.mids[n])
+                own[...] = (own[...].astype(F32) + self.mid[n].astype(F32)).astype(BF)
+                self.merged[n].start()
+
+        def wait(self):
+            for ref, sem in self.outs:
+                arrived(ref, sem)
+
+        def drain(self):
+            for cp in self.far + self.plain + self.merged:
+                cp.wait_send()
+
+    def steps(i):
+        return jnp.where(i < 2, i + 2, 3 - i)
+
+    def z_dev(to):
+        return dev(x, y, to, c)
+
     c8_to = [(x, 2 * (z // 2) + s, 2 * c + yh, z % 2) for s in range(2)]
     c8_from = [(x, 2 * (z % 2) + s, 2 * yh + c, z // 2) for s in range(2)]
 
@@ -128,20 +177,65 @@
     def sf_src(y_, c_, s):
         return sf.at[:, ds((2 * s + c_) * 4 + (y_ // 2) * 2 + y_ % 2, CB)]
 
-    def sf_send(n, s):
+    def sf_row(s, r, q):
+        return sf_r.at[s, pl.ds(pl.multiple_of(r * RK + q * QR, QR), QR), :]
+
+    for n, s in enumerate((s0, s1)):
         dst, rs = sf_r.at[s, ds(r4, RK), :], sf_rs.at[r4 * 2 + s]
         pltpu.make_async_copy(sf_src(y, c, s), dst, rs).start()
-        for m, (y_, c_) in enumerate(peers):
-            send(remote(sf_src(y_, c_, s), dst, sf_ss.at[m * 2 + n], rs, dev(x, y_, z, c_)))
-
-    def fx_send(k):
+        send(remote(sf_src(y, 1 - c, s), dst, sf_ss.at[n], rs, dev(x, y, z, 1 - c)))
+    for m, (y_, c_) in enumerate(peers[1:]):
+        src = sf_src(y_, c_, s0).at[ds(z, QR), :]
+        send(remote(src, sf_row(s0, r4, z), sf_ss.at[2 + m], sq_rs.at[r4 * 4 + z], dev(x, y_, z, c_)))
+
+    def sf_far():
+        for m, (y_, c_) in enumerate(peers[1:]):
+            dst, rs = sf_r.at[s1, ds(r4, RK), :], sf_rs.at[r4 * 2 + s1]
+            send(remote(sf_src(y_, c_, s1), dst, sf_ss.at[4 + m], rs, dev(x, y_, z, c_)))
+
+    def sf_onward():
+        for m in range(2):
+            r = (1 - yh) * 2 + m
+            unit, rs = sf_row(s0, r, z), sq_rs.at[r * 4 + z]
+            arrived(unit, rs)
+            for k in (2, 1, 3):
+                send(remote(unit, unit, sf_ss.at[6 + m * 3 + k - 1], rs, z_dev((z + k) % 4)))
+
+    def sf_wait_s0():
+        for m in range(2):
+            r = yh * 2 + m
+            arrived(sf_r.at[s0, ds(r, RK), :], sf_rs.at[r * 2 + s0])
+            r = (1 - yh) * 2 + m
+            for k in range(1, 4):
+                q = (z + k) % 4
+                arrived(sf_row(s0, r, q), sq_rs.at[r * 4 + q])
+
+    for k in range(4):
+        dst = ffx.at[k, :, ds(r4, RK)]
+        pltpu.make_async_copy(ff.at[k, r4], dst, fx_rs.at[k * 4 + r4]).start()
+        send(remote(ff.at[k, yh * 2 + 1 - c], dst, fx_ss.at[k], fx_rs.at[k * 4 + r4], dev(x, y, z, 1 - c)))
+    x_far = (x + 2 + z % 2) % 4
+
+    def fx_half(to, h, r):
+        return ffx.at[to, ds(h, FB // 2), ds(r, RK)]
+
+    for m, (y_, c_) in enumerate(peers[1:]):
+        src = ff.at[x_far, (y_ // 2) * 2 + c_, ds(z // 2, FB // 2)]
+        send(remote(src, fx_half(x_far, z // 2, r4), fx_ss.at[4 + m], fxh_rs.at[z * 4 + r4], dev(x, y_, z, c_)))
+
+    def fx_onward():
+        for m in range(2):
+            r = (1 - yh) * 2 + m
+            unit, rs = fx_half(x_far, z // 2, r), fxh_rs.at[z * 4 + r]
+            arrived(unit, rs)
+            for k in (2, 1, 3):
+                send(remote(unit, unit, fx_ss.at[6 + m * 3 + k - 1], rs, z_dev((z + k) % 4)))
+
+    def fx_near(k):
         to = (x + k) % 4
-        dst, rs = ffx.at[to, :, ds(r4, RK)], fx_rs.at[to * 4 + r4]
-        pltpu.make_async_copy(ff.at[to, r4], dst, rs).start()
-        for m, (y_, c_) in enumerate(peers):
-            send(remote(ff.at[to, (y_ // 2) * 2 + c_], dst, fx_ss.at[m * 4 + k], rs, dev(x, y_, z, c_)))
-
-    sf_send(0, s0)
+        for m, (y_, c_) in enumerate(peers[1:]):
+            dst, rs = ffx.at[to, :, ds(r4, RK)], fx_rs.at[to * 4 + r4]
+            send(remote(ff.at[to, (y_ // 2) * 2 + c_], dst, fx_ss.at[12 + k * 2 + m], rs, dev(x, y_, z, c_)))
 
     h_acc[...] = jnp.zeros_like(h_acc)
     for k in range(4):
@@ -159,9 +253,9 @@
         other = (line + j) % 8
         send(remote(ht_mine, ht_mine, h_ss.at[j], h_rs.at[line], dev(x, other // 2, z, other % 2)))
 
-    sf_send(1, s1)
-    fx_send(2)
-    fx_send(1)
+    sf_far()
+    sf_onward()
+    fx_near(1)
 
     rg_acc[...] = jnp.zeros_like(rg_acc)
 
@@ -179,20 +273,15 @@
 
         lax.fori_loop(0, 2, step, 0)
 
-    def sg_copy(k, s):
-        q = (z + k) % 4
-        return remote(sg_p.at[s, q], sg_r.at[s, z], sg_ss.at[k * 2 + s], sg_rs.at[z * 2 + s], dev(x, y, q, c))
-
-    def sg_block(s):
+    sgs = {}
+    for name, s in (("s0", s0), ("s1", s1)):
+        sgs[name] = RingSum(z, z_dev, lambda q, s=s: sg_p.at[s, q], RK, sg_m.at[s], sg_r.at[s], sg_ss, sg_rs, s * 6)
+
+    def sg_block(name, s):
         def step(i, _):
-            k = (i + 2) % 4
-            q = (z + k) % 4
+            q = (z + steps(i)) % 4
             sg_p[s, q] = nn(ht[ds(q, RK), :], og_r[s]).astype(BF)
-
-            @pl.when(k != 0)
-            def _():
-                sg_copy(k, s).start()
-
+            sgs[name].part_done(i)
             return 0
 
         lax.fori_loop(0, 4, step, 0)
@@ -215,10 +304,9 @@
     onward(0, *order[0])
     block(*order[1])
     onward(1, *order[1])
-    sf_wait(s0)
+    fx_onward()
+    sf_wait_s0()
     rg_block(*order[0])
-    sf_wait(s1)
-    rg_block(*order[1])
     for j in range(1, 8):
         other = (line + j) % 8
         y_, c_ = other // 2, other % 2
@@ -226,14 +314,22 @@
 
     @pl.when(root)
     def _():
-        sg_block(s0)
+        sg_block("s0", s0)
 
     block(*order[2])
     onward(2, *order[2])
-    rg_block(*order[2])
+    rg_block(s0, 1 - yl)
+
+    @pl.when(jnp.logical_not(root))
+    def _():
+        sg_block("s0", s0)
+
+    sgs["s0"].merge()
     block(*order[3])
     onward(3, *order[3])
-    rg_block(*order[3])
+    sf_wait(s1)
+    rg_block(s1, yl)
+    rg_block(s1, 1 - yl)
 
     for t in range(2):
         for n in range(2):
@@ -248,11 +344,8 @@
             )
         )
 
-    @pl.when(jnp.logical_not(root))
-    def _():
-        sg_block(s0)
-
-    sg_block(s1)
+    fx_near(0)
+    sg_block("s1", s1)
 
     total = rg_p[yl, :, ds(r4, RK)].astype(F32)
     for j in range(1, 8):
@@ -264,8 +357,6 @@
     for n, (y_, c_) in enumerate([(y, 1 - c), ((y + 2) % 4, 0), ((y + 2) % 4, 1)]):
         send(remote(rg_mine, rg_mine, ra_ss.at[n], ra_rs.at[r4], dev(x, y_, z, c_)))
     rgt[...] = total.T.astype(BF)
-    fx_send(3)
-    fx_send(0)
 
     def fg_unit(own, z_, half):
         u = (pick_yl(own) * 4 + z_) * 2 + half
@@ -275,9 +366,13 @@
     def pick_yl(own):
         return yl if own else 1 - yl
 
-    def z_copy(kind, u, k):
-        to = (z + k) % 4
-        return remote(fg_p.at[u], fg_z.at[kind, z], fz_ss.at[kind * 4 + k], fz_rs.at[kind * 4 + z], dev(x, y, to, c))
+    fgs = [
+        RingSum(
+            z, z_dev, lambda z_, n=n, o=o: fg_p.at[(pick_yl(o) * 4 + z_) * 2 + n // 2], RK,
+            fg_m.at[n], fg_z.at[n], fz_ss, fz_rs, n * 6,
+        )
+        for n, o in ((0, True), (1, False), (2, True))
+    ]
 
     def y_copy(u, z_):
         return remote(fg_p.at[u], fg_y.at[z_], fy_ss.at[z_], fy_rs.at[z_], dev(x, yp, z, c))
@@ -289,18 +384,15 @@
 
     lax.fori_loop(0, 4, p2, 0)
     for own in (False, True):
-
-        def first(i, _, own=own):
-            k = (i + 2) % 4
-            u = fg_unit(own, (z + k) % 4, 0)
-
-            @pl.when(k != 0)
-            def _():
-                z_copy(0 if own else 1, u, k).start()
-
+        zs = fgs[0 if own else 1]
+
+        def first(i, _, own=own, zs=zs):
+            fg_unit(own, (z + steps(i)) % 4, 0)
+            zs.part_done(i)
             return 0
 
         lax.fori_loop(0, 4, first, 0)
+    sgs["s1"].merge()
 
     def o2(z_, _):
         fg_unit(True, z_, 1)
@@ -312,69 +404,62 @@
         other = (r4 + j) % 4
         arrived(rg_all.at[:, ds(other, RK)], ra_rs.at[other])
 
-    def ig_copy(k):
-        to = (x + k) % 4
-        return remote(ig_p.at[to], ig_r.at[x], ig_ss.at[k], ig_rs.at[x], dev(to, y, z, c))
-
-    def ig_part(k):
-        to = (x + k) % 4
+    igs = RingSum(x, lambda to: dev(to, y, z, c), lambda x_: ig_p.at[x_], TOK, ig_m, ig_r, ig_ss, ig_rs, 0)
+
+    def ig_part(i, _):
+        to = (x + steps(i)) % 4
         for j in range(4):
-            arrived(ffx.at[to, :, j * RK : (j + 1) * RK], fx_rs.at[to * 4 + j])
+
+            @pl.when((i >= 2) | (j // 2 == yh))
+            def _(j=j):
+                arrived(ffx.at[to, :, j * RK : (j + 1) * RK], fx_rs.at[to * 4 + j])
+
+            for h in range(2):
+
+                @pl.when((i < 2) & (j // 2 != yh) & (i + 2 * h != z))
+                def _(j=j, h=h):
+                    arrived(fx_half(to, h, j), fxh_rs.at[(i + 2 * h) * 4 + j])
+
         ig_p[to] = nt(rg_all[...], ffx[to]).astype(BF)
-        if k:
-            send(ig_copy(k))
-
-    ig_part(2)
-    ig_part(1)
-
-    def merge(i, _):
-        k = (i + 2) % 4
-        z_ = (z + k) % 4
-        u = (yl * 4 + z_) * 2 + 1
-        arrived(fg_y.at[z_], fy_rs.at[z_])
-        fg_p[u] = (fg_p[u].astype(F32) + fg_y[z_].astype(F32)).astype(BF)
-
-        @pl.when(k != 0)
-        def _():
-            z_copy(2, u, k).start()
-
+        igs.part_done(i)
         return 0
 
-    lax.fori_loop(0, 4, merge, 0)
-    ig_part(3)
-    ig_part(0)
-
+    lax.fori_loop(0, 4, ig_part, 0)
+    fgs[1].merge()
+    fgs[0].merge()
+    igs.merge()
+
+    for zs in sgs.values():
+        zs.wait()
     for s in range(2):
-        for j in range(1, 4):
-            other = (z + j) % 4
-            arrived(sg_r.at[s, other], sg_rs.at[other * 2 + s])
-        total = sg_p[s, z].astype(F32)
-        for j in range(1, 4):
-            total = total + sg_r[s, (z + j) % 4].astype(F32)
-        sg_s[s] = total.astype(BF)
+        sg_s[s] = (sg_p[s, z].astype(F32) + sg_r[s, 0].astype(F32) + sg_r[s, 1].astype(F32)).astype(BF)
         dst = sg_out.at[:, ds(yl, CB)]
         near = pltpu.make_async_copy(sg_s.at[s], dst, c8_rs.at[yl])
         send(remote(sg_s.at[s], dst, c8_ss.at[s], c8_rs.at[yl], dev(*c8_to[s])), jnp.logical_not(is_me(c8_to[s])))
         pl.when(is_me(c8_to[s]))(near.start)
 
-    for j in range(1, 4):
-        other = (z + j) % 4
-        arrived(fg_z.at[1, other], fz_rs.at[4 + other])
-    total = fg_p[((1 - yl) * 4 + z) * 2].astype(F32)
-    for j in range(1, 4):
-        total = total + fg_z[1, (z + j) % 4].astype(F32)
+    def merge(i, _):
+        z_ = (z + steps(i)) % 4
+        u = (yl * 4 + z_) * 2 + 1
+        arrived(fg_y.at[z_], fy_rs.at[z_])
+        fg_p[u] = (fg_p[u].astype(F32) + fg_y[z_].astype(F32)).astype(BF)
+        fgs[2].part_done(i)
+        return 0
+
+    lax.fori_loop(0, 4, merge, 0)
+
+    fgs[1].wait()
+    total = fg_p[((1 - yl) * 4 + z) * 2].astype(F32) + fg_z[1, 0].astype(F32) + fg_z[1, 1].astype(F32)
     fg_f[0] = total.astype(BF)
     send(remote(fg_f.at[0], fg_f.at[1], ff_ss.at[0], ff_rs.at[0], dev(x, yp, z, c)))
-
-    for j in range(1, 4):
-        other = (x + j) % 4
-        arrived(ig_r.at[other], ig_rs.at[other])
+    fgs[2].merge()
+
+
+    igs.wait()
 
     def ig_sum(k, _):
         rows = ds(k, 64)
-        acc = ig_p[x, rows, :].astype(F32)
-        for j in range(1, 4):
-            acc = acc + ig_r[(x + j) % 4, rows, :].astype(F32)
+        acc = ig_p[x, rows, :].astype(F32) + ig_r[0, rows, :].astype(F32) + ig_r[1, rows, :].astype(F32)
         ig_out[rows, :] = acc.astype(BF)
         return 0
 
@@ -382,17 +467,15 @@
 
     for half in range(2):
         kind = 2 * half
-        for j in range(1, 4):
-            other = (z + j) % 4
-            arrived(fg_z.at[kind, other], fz_rs.at[kind * 4 + other])
+        fgs[kind].wait()
         if half == 0:
             arrived(fg_f.at[1], ff_rs.at[0])
 
         def fg_sum(k, _, half=half, kind=kind):
             cols = ds(k, 256)
             acc = fg_p[d * 2 + half, :, cols].astype(F32)
-            for j in range(1, 4):
-                acc = acc + fg_z[kind, (z + j) % 4, :, cols].astype(F32)
+            for j in range(2):
+                acc = acc + fg_z[kind, j, :, cols].astype(F32)
             if half == 0:
                 acc = acc + fg_f[1, :, cols].astype(F32)
             fg_out[ds(half * 4 + k, 256), :] = acc.T.astype(BF)
@@ -408,15 +491,16 @@
             cp.wait_send()
         else:
             pl.when(cond)(cp.wait_send)
-    for k in range(1, 4):
-        for s in range(2):
-            sg_copy(k, s).wait_send()
-        z_ = (z + k) % 4
-        z_copy(0, (yl * 4 + z_) * 2, k).wait_send()
-        z_copy(1, ((1 - yl) * 4 + z_) * 2, k).wait_send()
-        z_copy(2, (yl * 4 + z_) * 2 + 1, k).wait_send()
+    for zs in list(sgs.values()) + fgs + [igs]:
+        zs.drain()
     for z_ in range(4):
         y_copy(((1 - yl) * 4 + z_) * 2 + 1, z_).wait_send()
+
+
+def place(a, b, c, a_out, b_out, c_out):
+    a_out[...] = a[...]
+    b_out[...] = b[...]
+    c_out[...] = c[...]
 
 
 def shards(inputs, first_factor, second_factor, out_grad):
@@ -424,7 +508,7 @@
     any_ = pl.BlockSpec(memory_space=pl.ANY)
     vmem = pl.BlockSpec(memory_space=pltpu.VMEM)
     dma = pltpu.SemaphoreType.DMA
-    return pl.pallas_call(
+    results = pl.pallas_call(
         kernel,
         name="backward",
         out_shape=(
@@ -447,34 +531,44 @@
             pltpu.VMEM((8, TOK, RK), BF),
             pltpu.VMEM((TOK, 4 * RK), BF),
             pltpu.VMEM((2, 4, RK, CB), BF),
-            pltpu.VMEM((2, 4, RK, CB), BF),
+            pltpu.VMEM((2, 2, RK // 2, CB), BF),
+            pltpu.VMEM((2, 2, RK, CB), BF),
             pltpu.VMEM((2, RK, CB), BF),
             pltpu.VMEM((16, RK, FB), BF),
             pltpu.VMEM((4, RK, FB), BF),
-            pltpu.VMEM((3, 4, RK, FB), BF),
+            pltpu.VMEM((3, 2, RK // 2, FB), BF),
+            pltpu.VMEM((3, 2, RK, FB), BF),
             pltpu.VMEM((2, RK, FB), BF),
             pltpu.VMEM((4, TOK, FB), BF),
-            pltpu.VMEM((4, TOK, FB), BF),
+            pltpu.VMEM((2, TOK // 2, FB), BF),
+            pltpu.VMEM((2, TOK, FB), BF),
             pltpu.VMEM((RK, TOK), BF),
             dma((4,)), dma((4,)),
             dma((4,)), dma((4,)), dma((8,)),
-            dma((6,)), dma((8,)),
-            dma((12,)), dma((16,)),
+            dma((12,)), dma((8,)), dma((16,)),
+            dma((16,)), dma((16,)), dma((16,)),
             dma((8,)), dma((8,)),
             dma((8,)), dma((8,)),
             dma((3,)), dma((4,)),
-            dma((8,)), dma((8,)),
+            dma((12,)), dma((12,)),
             dma((2,)), dma((2,)),
             dma((4,)), dma((4,)),
-            dma((12,)), dma((12,)),
+            dma((18,)), dma((18,)),
             dma((1,)), dma((1,)),
-            dma((4,)), dma((4,)),
+            dma((6,)), dma((6,)),
         ],
         cost_estimate=pl.CostEstimate(flops=10_100_000_000, bytes_accessed=30_000_000, transcendentals=0),
         compiler_params=pltpu.CompilerParams(
             collective_id=0, has_side_effects=True, vmem_limit_bytes=63 * 1024 * 1024
         ),
     )(inputs, ff, second_factor, out_grad)
+    return pl.pallas_call(
+        place,
+        name="place",
+        out_shape=[jax.ShapeDtypeStruct(r.shape, r.dtype) for r in results],
+        in_specs=[vmem] * 3,
+        out_specs=[vmem] * 3,
+    )(*results)
 
 
 def solution(mesh):

time: 160 us -> 147 us (0.919)
  the two profiles are of different devices: /device:TPU:3 before, /device:TPU:5 now
where the time goes in v3:
time: 147 us; the launch traced here: 144 us
  Pallas kernels  144 us (98%)
    pallas_call x1, Pallas kernels, shards(): pl.pallas_call(kernel, name='backward', out_shape=(jax.ShapeDtypeStruct((...  141 us

profile of v3, /device:TPU:5, one launch (start us, length us, event | category | flops | bytes accessed | tf_op | source)
XLA Modules:
  0.0 144.2 jit_solution(10928726591878372769)
XLA Ops:
  0.6 140.7 %backward.1 = (bf16[384,1024]{1,0:T(8,128)(2,1)}, bf16[2048,128]{1,0:T(8,128)(2,1)}, bf16[128,3328]{1,0:T(8,128)(2,1)}) custom-call(bf16[384,16384]{1,0:T(8,128)(2,1)} %inp.1, bf16[4,4,1024,128]{3,2,1,0:T(8,128)(2,1)} %bitcast.1, bf16[128,26624]{1,0:T(8,128)(2,1)} %sf.1, bf16[384,1664]{1,0:T(8,128)(2,1)} %og.1), custom_call_target="tpu_custom_call" | custom-call | flops 10099999744 | bytes 30000000 | tf_op jit(solution)/shard_map/backward/pallas_call | solution.py:511
  141.3 2.9 %place.1 = (bf16[384,1024]{1,0:T(8,128)(2,1)}, bf16[2048,128]{1,0:T(8,128)(2,1)}, bf16[128,3328]{1,0:T(8,128)(2,1)}) custom-call(bf16[384,1024]{1,0:T(8,128)(2,1)} %get-tuple-element.6.a, bf16[2048,128]{1,0:T(8,128)(2,1)} %get-tuple-element.7.b, bf16[128,3328]{1,0:T(8,128)(2,1)} %get-tuple-element.8.c), custom_call_target="tpu_custom_call" | custom-call | tf_op jit(solution)/shard_map/place/pallas_call | solution.py:565

commit v4 on v3

--- a/solution.py
+++ b/solution.py
@@ -347,6 +347,17 @@
     fx_near(0)
     sg_block("s1", s1)
 
+    def c8_send(name, s):
+        sgs[name].wait()
+        sg_s[s] = (sg_p[s, z].astype(F32) + sg_r[s, 0].astype(F32) + sg_r[s, 1].astype(F32)).astype(BF)
+        dst = sg_out.at[:, ds(yl, CB)]
+        to = (x, 2 * (z // 2) + s, 2 * c + yh, z % 2)
+        near = pltpu.make_async_copy(sg_s.at[s], dst, c8_rs.at[yl])
+        send(remote(sg_s.at[s], dst, c8_ss.at[s], c8_rs.at[yl], dev(*to)), jnp.logical_not(is_me(to)))
+        pl.when(is_me(to))(near.start)
+
+    c8_send("s0", s0)
+
     total = rg_p[yl, :, ds(r4, RK)].astype(F32)
     for j in range(1, 8):
         other = (line + j) % 8
@@ -383,6 +394,7 @@
         return 0
 
     lax.fori_loop(0, 4, p2, 0)
+    sgs["s1"].merge()
     for own in (False, True):
         zs = fgs[0 if own else 1]
 
@@ -392,7 +404,6 @@
             return 0
 
         lax.fori_loop(0, 4, first, 0)
-    sgs["s1"].merge()
 
     def o2(z_, _):
         fg_unit(True, z_, 1)
@@ -427,16 +438,9 @@
     lax.fori_loop(0, 4, ig_part, 0)
     fgs[1].merge()
     fgs[0].merge()
+    c8_send("s1", s1)
+
     igs.merge()
-
-    for zs in sgs.values():
-        zs.wait()
-    for s in range(2):
-        sg_s[s] = (sg_p[s, z].astype(F32) + sg_r[s, 0].astype(F32) + sg_r[s, 1].astype(F32)).astype(BF)
-        dst = sg_out.at[:, ds(yl, CB)]
-        near = pltpu.make_async_copy(sg_s.at[s], dst, c8_rs.at[yl])
-        send(remote(sg_s.at[s], dst, c8_ss.at[s], c8_rs.at[yl], dev(*c8_to[s])), jnp.logical_not(is_me(c8_to[s])))
-        pl.when(is_me(c8_to[s]))(near.start)
 
     def merge(i, _):
         z_ = (z + steps(i)) % 4

time: 147 us -> 144 us (0.980); the launches traced: 144 us -> 144 us
  no operation moved by 1% of the time
where the time goes in v4:
time: 144 us
  Pallas kernels  143 us (99%)
    pallas_call x1, Pallas kernels, shards(): pl.pallas_call(kernel, name='backward', out_shape=(jax.ShapeDtypeStruct((...  140 us
    pallas_call x1, Pallas kernels, shards(): pl.pallas_call(place, name='place', out_shape=[jax.ShapeDtypeStruct(r.sha...  2.92 us

profile of v4, /device:TPU:5, one launch (start us, length us, event | category | flops | bytes accessed | tf_op | source)
XLA Modules:
  0.0 144.0 jit_solution(9689648608924761828)
XLA Ops:
  0.6 140.4 %backward.1 = (bf16[384,1024]{1,0:T(8,128)(2,1)}, bf16[2048,128]{1,0:T(8,128)(2,1)}, bf16[128,3328]{1,0:T(8,128)(2,1)}) custom-call(bf16[384,16384]{1,0:T(8,128)(2,1)} %inp.1, bf16[4,4,1024,128]{3,2,1,0:T(8,128)(2,1)} %bitcast.1, bf16[128,26624]{1,0:T(8,128)(2,1)} %sf.1, bf16[384,1664]{1,0:T(8,128)(2,1)} %og.1), custom_call_target="tpu_custom_call" | custom-call | flops 10099999744 | bytes 30000000 | tf_op jit(solution)/shard_map/backward/pallas_call | solution.py:515
  141.0 2.9 %place.1 = (bf16[384,1024]{1,0:T(8,128)(2,1)}, bf16[2048,128]{1,0:T(8,128)(2,1)}, bf16[128,3328]{1,0:T(8,128)(2,1)}) custom-call(bf16[384,1024]{1,0:T(8,128)(2,1)} %get-tuple-element.6.a, bf16[2048,128]{1,0:T(8,128)(2,1)} %get-tuple-element.7.b, bf16[128,3328]{1,0:T(8,128)(2,1)} %get-tuple-element.8.c), custom_call_target="tpu_custom_call" | custom-call | tf_op jit(solution)/shard_map/place/pallas_call | solution.py:569

commit v5 on v4

--- a/solution.py
+++ b/solution.py
@@ -289,24 +289,27 @@
     def pick(u, v):
         return jnp.where(root, u, v)
 
-    def onward(i, s, t):
-        src = og_r.at[s, ds(t, TOK), :]
+    def onward_root():
+        src, rs = og_r.at[s0, ds(1 - yl, TOK), :], og_rs.at[s0 * 2 + 1 - yl]
+        send(remote(src, src, fwd_ss.at[0], rs, dev(right, y, z, c)), root)
+        send(remote(src, src, fwd_ss.at[1], rs, dev(left, y, z, c)), root)
+
+    leaf = jnp.logical_not(root)
+
+    def onward_leaf(i, s, t):
+        src, rs = og_r.at[s, ds(t, TOK), :], og_rs.at[s * 2 + t]
         from_left = (2 * s + c) == left
-        mine = root & (s == s0) & (t != yl)
-        ahead = jnp.logical_not(root) & (t == 0) & from_left
-        back = jnp.logical_not(root) & (t == 1) & jnp.logical_not(from_left)
-        rs = og_rs.at[s * 2 + t]
-        send(remote(src, src, fwd_ss.at[i * 2], rs, dev(right, y, z, c)), mine | ahead)
-        send(remote(src, src, fwd_ss.at[i * 2 + 1], rs, dev(left, y, z, c)), mine | back)
-
-    order = [(s0, yl), (pick(s0, s1), pick(1 - yl, yl)), (pick(s1, s0), pick(yl, 1 - yl)), (s1, 1 - yl)]
-    block(*order[0])
-    onward(0, *order[0])
-    block(*order[1])
-    onward(1, *order[1])
+        ahead = leaf & (t == 0) & from_left
+        back = leaf & (t == 1) & jnp.logical_not(from_left)
+        send(remote(src, src, fwd_ss.at[2 + i * 2], rs, dev(right, y, z, c)), ahead)
+        send(remote(src, src, fwd_ss.at[3 + i * 2], rs, dev(left, y, z, c)), back)
+
+    block(s0, yl)
+    block(pick(s0, s1), pick(1 - yl, yl))
+    onward_root()
     fx_onward()
     sf_wait_s0()
-    rg_block(*order[0])
+    rg_block(s0, yl)
     for j in range(1, 8):
         other = (line + j) % 8
         y_, c_ = other // 2, other % 2
@@ -315,18 +318,36 @@
     @pl.when(root)
     def _():
         sg_block("s0", s0)
-
-    block(*order[2])
-    onward(2, *order[2])
-    rg_block(s0, 1 - yl)
-
-    @pl.when(jnp.logical_not(root))
+        rg_block(s0, 1 - yl)
+        sgs["s0"].merge()
+
+    @pl.when(leaf)
+    def _():
+        block(s0, 1 - yl)
+
+    onward_leaf(0, s0, yl)
+    onward_leaf(1, s1, yl)
+    onward_leaf(2, s0, 1 - yl)
+
+    @pl.when(leaf)
     def _():
         sg_block("s0", s0)
-
-    sgs["s0"].merge()
-    block(*order[3])
-    onward(3, *order[3])
+        block(s1, 1 - yl)
+
+    onward_leaf(3, s1, 1 - yl)
+
+    @pl.when(leaf)
+    def _():
+        sg_block("s1", s1)
+        rg_block(s0, 1 - yl)
+        sgs["s0"].merge()
+        sgs["s1"].merge()
+
+    @pl.when(root)
+    def _():
+        block(s1, yl)
+        block(s1, 1 - yl)
+
     sf_wait(s1)
     rg_block(s1, yl)
     rg_block(s1, 1 - yl)
@@ -345,7 +366,11 @@
         )
 
     fx_near(0)
-    sg_block("s1", s1)
+
+    @pl.when(root)
+    def _():
+        sg_block("s1", s1)
+
 
     def c8_send(name, s):
         sgs[name].wait()
@@ -394,7 +419,7 @@
         return 0
 
     lax.fori_loop(0, 4, p2, 0)
-    sgs["s1"].merge()
+    pl.when(root)(sgs["s1"].merge)
     for own in (False, True):
         zs = fgs[0 if own else 1]
 
@@ -548,7 +573,7 @@
             pltpu.VMEM((2, TOK, FB), BF),
             pltpu.VMEM((RK, TOK), BF),
             dma((4,)), dma((4,)),
-            dma((4,)), dma((4,)), dma((8,)),
+            dma((4,)), dma((4,)), dma((10,)),
             dma((12,)), dma((8,)), dma((16,)),
             dma((16,)), dma((16,)), dma((16,)),
             dma((8,)), dma((8,)),

time: 144 us -> 130 us (0.903)
  Pallas kernels: 143 us -> 129 us
    pallas_call x1, Pallas kernels: 140 us -> 126 us  [shards(): pl.pallas_call(kernel, name='backward', out_shape=(jax.ShapeDtypeStruct((...]
where the time goes in v5:
time: 130 us; the launch traced here: 129 us
  Pallas kernels  129 us (99%)
    pallas_call x1, Pallas kernels, shards(): pl.pallas_call(kernel, name='backward', out_shape=(jax.ShapeDtypeStruct((...  126 us
    pallas_call x1, Pallas kernels, shards(): pl.pallas_call(place, name='place', out_shape=[jax.ShapeDtypeStruct(r.sha...  2.92 us

profile of v5, /device:TPU:5, one launch (start us, length us, event | category | flops | bytes accessed | tf_op | source)
XLA Modules:
  0.0 129.3 jit_solution(13195251952964731378)
XLA Ops:
  0.6 125.8 %backward.1 = (bf16[384,1024]{1,0:T(8,128)(2,1)}, bf16[2048,128]{1,0:T(8,128)(2,1)}, bf16[128,3328]{1,0:T(8,128)(2,1)}) custom-call(bf16[384,16384]{1,0:T(8,128)(2,1)} %inp.1, bf16[4,4,1024,128]{3,2,1,0:T(8,128)(2,1)} %bitcast.1, bf16[128,26624]{1,0:T(8,128)(2,1)} %sf.1, bf16[384,1664]{1,0:T(8,128)(2,1)} %og.1), custom_call_target="tpu_custom_call" | custom-call | flops 10099999744 | bytes 30000000 | tf_op jit(solution)/shard_map/backward/pallas_call | solution.py:540
  126.4 2.9 %place.1 = (bf16[384,1024]{1,0:T(8,128)(2,1)}, bf16[2048,128]{1,0:T(8,128)(2,1)}, bf16[128,3328]{1,0:T(8,128)(2,1)}) custom-call(bf16[384,1024]{1,0:T(8,128)(2,1)} %get-tuple-element.6.a, bf16[2048,128]{1,0:T(8,128)(2,1)} %get-tuple-element.7.b, bf16[128,3328]{1,0:T(8,128)(2,1)} %get-tuple-element.8.c), custom_call_target="tpu_custom_call" | custom-call | tf_op jit(solution)/shard_map/place/pallas_call | solution.py:594

commit v6 on v5

--- a/solution.py
+++ b/solution.py
@@ -349,22 +349,25 @@
         block(s1, 1 - yl)
 
     sf_wait(s1)
-    rg_block(s1, yl)
-    rg_block(s1, 1 - yl)
-
-    for t in range(2):
+    def rg_send(t, first):
         for n in range(2):
             rg_p[t, :, n * 256 : (n + 1) * 256] = rg_acc[t, n].astype(BF)
-    for j in range(1, 8):
-        other = (line + j) % 8
-        y_, c_ = other // 2, other % 2
-        send(
-            remote(
-                rg_p.at[y_ % 2, :, ds((y_ // 2) * 2 + c_, RK)], rg_r.at[line], rg_ss.at[j], rg_rs.at[line],
-                dev(x, y_, z, c_),
-            )
-        )
-
+        for yy in range(2):
+            for cc in range(2):
+                if first or yy or cc:
+                    y_ = 2 * ((yh + yy) % 2) + t
+                    c_ = (c + cc) % 2
+                    send(
+                        remote(
+                            rg_p.at[t, :, ds((y_ // 2) * 2 + c_, RK)], rg_r.at[line],
+                            rg_ss.at[first * 4 + yy * 2 + cc], rg_rs.at[line], dev(x, y_, z, c_),
+                        )
+                    )
+
+    rg_block(s1, 1 - yl)
+    rg_send(1 - yl, 1)
+    rg_block(s1, yl)
+    rg_send(yl, 0)
     fx_near(0)
 
     @pl.when(root)
@@ -381,7 +384,6 @@
         send(remote(sg_s.at[s], dst, c8_ss.at[s], c8_rs.at[yl], dev(*to)), jnp.logical_not(is_me(to)))
         pl.when(is_me(to))(near.start)
 
-    c8_send("s0", s0)
 
     total = rg_p[yl, :, ds(r4, RK)].astype(F32)
     for j in range(1, 8):
@@ -435,6 +437,7 @@
         return 0
 
     lax.fori_loop(0, 4, o2, 0)
+    c8_send("s0", s0)
 
     for j in range(1, 4):
         other = (r4 + j) % 4

time: 130 us -> 128 us (0.985)
  Pallas kernels: 129 us -> 126 us
    pallas_call x1, Pallas kernels: 126 us -> 123 us  [shards(): pl.pallas_call(kernel, name='backward', out_shape=(jax.ShapeDtypeStruct((...]
where the time goes in v6:
time: 128 us; the launch traced here: 127 us
  Pallas kernels  126 us (98%)
    pallas_call x1, Pallas kernels, shards(): pl.pallas_call(kernel, name='backward', out_shape=(jax.ShapeDtypeStruct((...  123 us
    pallas_call x1, Pallas kernels, shards(): pl.pallas_call(place, name='place', out_shape=[jax.ShapeDtypeStruct(r.sha...  2.92 us

profile of v6, /device:TPU:5, one launch (start us, length us, event | category | flops | bytes accessed | tf_op | source)
XLA Modules:
  0.0 126.7 jit_solution(14046517425359358003)
XLA Ops:
  0.6 123.2 %backward.1 = (bf16[384,1024]{1,0:T(8,128)(2,1)}, bf16[2048,128]{1,0:T(8,128)(2,1)}, bf16[128,3328]{1,0:T(8,128)(2,1)}) custom-call(bf16[384,16384]{1,0:T(8,128)(2,1)} %inp.1, bf16[4,4,1024,128]{3,2,1,0:T(8,128)(2,1)} %bitcast.1, bf16[128,26624]{1,0:T(8,128)(2,1)} %sf.1, bf16[384,1664]{1,0:T(8,128)(2,1)} %og.1), custom_call_target="tpu_custom_call" | custom-call | flops 10099999744 | bytes 30000000 | tf_op jit(solution)/shard_map/backward/pallas_call | solution.py:543
  123.8 2.9 %place.1 = (bf16[384,1024]{1,0:T(8,128)(2,1)}, bf16[2048,128]{1,0:T(8,128)(2,1)}, bf16[128,3328]{1,0:T(8,128)(2,1)}) custom-call(bf16[384,1024]{1,0:T(8,128)(2,1)} %get-tuple-element.6.a, bf16[2048,128]{1,0:T(8,128)(2,1)} %get-tuple-element.7.b, bf16[128,3328]{1,0:T(8,128)(2,1)} %get-tuple-element.8.c), custom_call_target="tpu_custom_call" | custom-call | tf_op jit(solution)/shard_map/place/pallas_call | solution.py:597
